TPU v7x, 256 devices: a whole 4x4x8 slice. The times are simulated.
256 devices in a mesh: tensor: 4 (over y_hi, core), dp: 64 (over z, y_lo, x).
Axes of the slice: x: 4, y: 4 (y_hi: 2, y_lo: 2; y = y_hi * 2 + y_lo), z: 8, core: 2. Of those that a mesh axis runs over, the one named last changes fastest.
Arguments:
- attn_out: bfloat16 [32768, 4096], P('dp', 'tensor'), may hold values from -6 to 6
- out_grad: bfloat16 [32768, 4096], P('dp', 'tensor'), may hold values from -0.21875 to 0.21875
- q_left: bfloat16 [4, 4, 1024, 1024], P('tensor', None, 'dp'), may hold values from -0.1875 to 0.1875
- q_right: bfloat16 [4, 1024, 1024], P('tensor', 'dp'), may hold values from -0.1875 to 0.1875
- weight: float32 [4096, 4096], P('dp', 'tensor'), may hold values from -6 to 6
- moment: float32 [4096, 4096], P(('tensor', 'dp')), may hold values from -6 to 6
- second: float32 [4096, 4096], P(('tensor', 'dp')), may hold values from 0.25 to 4
Outputs:
- new_weight: float32 [4096, 4096], P('dp', 'tensor')
- update: bfloat16 [4096, 4096], P('dp', 'tensor')
- new_moment: float32 [4096, 4096], P(('tensor', 'dp'))
- new_second: float32 [4096, 4096], P(('tensor', 'dp'))
All inputs are finite; a program needn't handle non-finite values.
Results may differ from a plain program's by a relative error of at most 0.001.
Values may be sent and summed in bfloat16 or wider, within the bound.
No kernel may reach another device: no remote copies, remote signals or barrier semaphores. Data moves between devices by JAX's collectives and lax.ppermute only.
A program may use at most 128 MiB of HBM per device.

v0:
```python
import jax
import jax.numpy as jnp
from jax import lax
from jax.sharding import PartitionSpec as P

STEP = 10


beta_first = 0.9
beta_second = 0.95
adam_eps = 1e-08
learn_rate = 0.1
weight_decay = 0.1


def adam_step(moment, second, rotated):
    new_moment = beta_first * moment + (1.0 - beta_first) * rotated
    new_second = beta_second * second + (1.0 - beta_second) * rotated * rotated
    first_fix = 1.0 - beta_first**STEP
    second_fix = 1.0 - beta_second**STEP
    normed = new_moment / first_fix / (jnp.sqrt(new_second / second_fix) + adam_eps)
    return (new_moment, new_second, normed)


def local(attn_out, out_grad, q_left, q_right, weight, moment, second):
    dp_count = lax.axis_size("dp")
    in_width = attn_out.shape[1]
    in_rows = in_width // dp_count
    full_grad = lax.all_gather(out_grad, "tensor", axis=1, tiled=True)
    out_width = full_grad.shape[1]
    left_whole, right_whole = (
        lax.all_gather(q_left, "dp", axis=2, tiled=True),
        lax.all_gather(q_right, "dp", axis=1, tiled=True),
    )
    left_basis = left_whole[0].astype(jnp.float32)
    right_basis = right_whole[0].astype(jnp.float32)
    blocks = left_basis.shape[0]
    block_size = left_basis.shape[1]
    grad_cols = lax.psum_scatter(
        lax.dot_general(
            attn_out, full_grad, (((0,), (0,)), ((), ())), preferred_element_type=jnp.float32
        ),
        "dp",
        scatter_dimension=0,
        tiled=True,
    )
    left_done = jnp.einsum(
        "ibo,bop->ibp",
        grad_cols.reshape(in_rows, blocks, block_size),
        left_basis,
        precision=lax.Precision.HIGHEST,
    ).reshape(in_rows, out_width)
    left_rows = lax.all_to_all(left_done, "dp", split_axis=1, concat_axis=0, tiled=True)
    both_rows = lax.dot_general(
        left_rows, right_basis, (((0,), (0,)), ((), ())), precision=lax.Precision.HIGHEST
    )
    both_cols = lax.all_to_all(both_rows, "dp", split_axis=1, concat_axis=0, tiled=True)
    rotated = both_cols.T
    new_moment, new_second, normed = adam_step(moment, second, rotated)
    back_left = jnp.einsum(
        "ibp,bop->ibo",
        normed.reshape(in_rows, blocks, block_size),
        left_basis,
        precision=lax.Precision.HIGHEST,
    ).reshape(in_rows, out_width)
    back_rows = lax.all_to_all(back_left, "dp", split_axis=1, concat_axis=0, tiled=True)
    unrotated = lax.dot_general(
        back_rows, right_basis, (((0,), (1,)), ((), ())), precision=lax.Precision.HIGHEST
    )
    new_weight = weight - learn_rate * (unrotated + weight_decay * weight)
    return (new_weight, unrotated.astype(jnp.bfloat16), new_moment, new_second)


def solution(mesh):
    return jax.shard_map(
        local,
        mesh=mesh,
        in_specs=(
            P("dp", "tensor"),
            P("dp", "tensor"),
            P("tensor", None, "dp", None),
            P("tensor", "dp", None),
            P("dp", "tensor"),
            P(("tensor", "dp"), None),
            P(("tensor", "dp"), None),
        ),
        out_specs=(
            P("dp", "tensor"),
            P("dp", "tensor"),
            P(("tensor", "dp"), None),
            P(("tensor", "dp"), None),
        ),
        check_vma=False,
    )
```

profile of v0, /device:TPU:8, one launch (start us, length us, event | category | flops | bytes accessed | tf_op | source)
XLA Modules:
  0.0 1102.8 jit_solution(11722575191506164666)
XLA Ops:
  7.2 0.0 copy-start
  7.2 0.0 all-gather.4.cloned.1.call-start
  7.2 0.7 all-gather.4.cloned.1.call-update
  7.9 0.0 all-gather.6.cloned.1.call-start
  8.0 0.7 all-gather.6.cloned.1.call-update
  8.7 0.0 reduce-scatter.2.cloned.1.call-start
  8.7 44.2 %all-gather.4.cloned.1.call-done = bf16[512,4096]{1,0:T(8,128)(2,1)} async-done(((bf16[512,1024]{1,0:T(8,128)(2,1)}), bf16[512,4096]{1,0:T(8,128)(2,1)}) %all-gather.4.cloned.1.call-update) | async-done | bytes 4194320 | tf_op jit(solution)/shard_map/all_gather | solution.py:29
  52.9 0.0 copy-done
  52.9 10.3 fusion.23
  63.3 0.0 reduce-scatter.2.cloned.1.call-update
  63.3 0.0 all-gather.8.cloned.1.call-start
  63.3 0.5 all-gather.8.cloned.1.call-update
  63.9 299.4 %all-gather.6.cloned.1.call-done = bf16[1,4,1024,1024]{3,2,1,0:T(8,128)(2,1)} async-done(((bf16[1,4,16,1024]{3,2,1,0:T(8,128)(2,1)}), bf16[1,4,1024,1024]{3,2,1,0:T(8,128)(2,1)}) %all-gather.6.cloned.1.call-update) | async-done | bytes 8388624 | tf_op jit(solution)/shard_map/all_gather | solution.py:32
  363.2 352.3 %reduce-scatter.2.cloned.1.call-done = f32[16,4096]{1,0:T(8,128)} async-done(((f32[1024,4096]{1,0:T(8,128)}), f32[16,4096]{1,0:T(8,128)}) %reduce-scatter.2.cloned.1.call-update) | async-done | bytes 262160 | tf_op jit(solution)/shard_map/reduce_scatter | solution.py:39
  715.5 5.8 fusion.8
  721.3 0.2 copy.24
  721.5 0.2 all_to_all.40
  721.7 0.3 copy.51
  722.0 1.0 reshape.31
  723.1 13.4 %all-to-all-start = ((f32[64,1,1024]{2,1,0:T(1,128)}), f32[64,1,1024]{2,1,0:T(1,128)S(1)}, u32[]{:S(2)}, u32[]{:S(2)}) async-start(f32[64,1,1024]{2,1,0:T(1,128)} %reshape.31), calls=%async_computation.1 | async-start | bytes 524288 | tf_op jit(solution)/shard_map/all_to_all | solution.py:53
  736.5 280.8 %all-gather.8.cloned.1.call-done = bf16[1,1024,1024]{2,1,0:T(8,128)(2,1)} async-done(((bf16[1,16,1024]{2,1,0:T(8,128)(2,1)}), bf16[1,1024,1024]{2,1,0:T(8,128)(2,1)}) %all-gather.8.cloned.1.call-update) | async-done | bytes 2097168 | tf_op jit(solution)/shard_map/all_gather | solution.py:33
  1017.3 2.9 copy.26
  1020.2 0.0 all-to-all-done
  1020.2 0.0 copy-start.2
  1020.2 0.7 copy-done.2
  1020.9 0.5 broadcast.7
  1021.4 2.2 reduce
  1023.6 0.9 reshape.32
  1024.6 6.7 fusion.6
  1031.3 1.4 copy.29
  1032.7 0.3 reshape.33
  1033.0 23.3 %all_to_all.54 = f32[64,1,1024]{2,1,0:T(1,128)S(1)} all-to-all(f32[64,1,1024]{2,1,0:T(1,128)S(1)} %reshape.33), channel_id=1, replica_groups=mesh['tensor'=4,'dp'=64] {'dp'}, dimensions={0} | all-to-all | bytes 524288 | tf_op jit(solution)/shard_map/all_to_all | solution.py:57
  1056.3 1.3 reduce.1
  1057.6 0.1 reshape.34
  1057.8 0.2 copy.30
  1057.9 0.2 all_to_all.46
  1058.1 0.0 copy-done.3
  1058.1 0.9 add_divide_fusion
  1059.1 8.9 fusion.11
  1068.0 0.2 copy.32
  1068.2 1.0 all_to_all.47
  1069.2 2.1 copy.50
  1071.4 1.4 reshape.35
  1072.7 16.4 %all_to_all.55 = f32[64,1,1024]{2,1,0:T(1,128)} all-to-all(f32[64,1,1024]{2,1,0:T(1,128)S(1)} %reshape.35), channel_id=1, replica_groups=mesh['tensor'=4,'dp'=64] {'dp'}, dimensions={0} | all-to-all | bytes 524288 | tf_op jit(solution)/shard_map/all_to_all | solution.py:66
  1089.2 2.2 reduce.2
  1091.4 0.9 reshape.36
  1092.3 0.0 copy-done.1
  1092.3 3.9 fusion.22
  (5 shorter events, 0.0 us)
Async XLA Ops:
  7.2 45.8 %copy-start = (bf16[512,1024]{1,0:T(8,128)(2,1)S(1)}, bf16[512,1024]{1,0:T(8,128)(2,1)}, u32[]{:S(2)}) copy-start(bf16[512,1024]{1,0:T(8,128)(2,1)} %param.7) | copy-start | bytes 3145732
  7.2 45.8 %all-gather.4.cloned.1.call-start = ((), (), s32[]{:S(2)}) async-start(), calls=%async_computation.4 | async-start | bytes 5242880 | tf_op jit(solution)/shard_map/all_gather | solution.py:29
  7.9 355.3 %all-gather.6.cloned.1.call-start = ((), (), s32[]{:S(2)}) async-start(), calls=%async_computation.6 | async-start | bytes 8519680 | tf_op jit(solution)/shard_map/all_gather | solution.py:32
  8.7 706.8 %reduce-scatter.2.cloned.1.call-start = ((), (), s32[]{:S(2)}) async-start(), calls=%async_computation.5 | async-start | bytes 17039360 | tf_op jit(solution)/shard_map/reduce_scatter | solution.py:39
  63.3 954.0 %all-gather.8.cloned.1.call-start = ((), (), s32[]{:S(2)}) async-start(), calls=%async_computation.7 | async-start | bytes 2129920 | tf_op jit(solution)/shard_map/all_gather | solution.py:33
  723.1 297.1 %all-to-all-start = ((f32[64,1,1024]{2,1,0:T(1,128)}), f32[64,1,1024]{2,1,0:T(1,128)S(1)}, u32[]{:S(2)}, u32[]{:S(2)}) async-start(f32[64,1,1024]{2,1,0:T(1,128)} %reshape.31), calls=%async_computation.1 | async-start | bytes 524288 | tf_op jit(solution)/shard_map/all_to_all | solution.py:53
  1020.2 0.7 copy-start.2
  1024.6 33.6 %copy-start.3 = (f32[16,4096]{1,0:T(8,128)S(1)}, f32[16,4096]{1,0:T(8,128)}, u32[]{:S(2)}) copy-start(f32[16,4096]{1,0:T(8,128)} %param.12) | copy-start | bytes 786436
  1031.3 26.8 %copy-start.4 = (f32[16,4096]{1,0:T(8,128)S(1)}, f32[16,4096]{1,0:T(8,128)}, u32[]{:S(2)}) copy-start(f32[16,4096]{1,0:T(8,128)} %param.13) | copy-start | bytes 786436
  1068.0 24.4 %copy-start.1 = (bf16[1,1024,1024]{2,1,0:T(8,128)(2,1)S(1)}, bf16[1,1024,1024]{2,1,0:T(8,128)(2,1)}, u32[]{:S(2)}) copy-start(bf16[1,1024,1024]{2,1,0:T(8,128)(2,1)} %all-gather.8.cloned.1.call-done) | copy-start | bytes 6291460
Sparse Core Ops, SparseCore 0:
  9.8 43.0 all-gather.3
  54.7 308.4 all-gather.5
  365.8 349.6 reduce-scatter.1
  717.2 300.1 all-gather.7
where the time goes:
time: 1100 us
  waiting for transfers between devices  979 us (89%)
  blocking collectives  39.8 us (4%)
  matrix products  35.6 us (3%)
  local copies, waits for them, and re-layouts  14.7 us (1%)
  between operations  13.9 us (1%)
  starting transfers between devices  13.6 us (1%)
    reduce_scatter x1, waiting for transfers between devices, local(): lax.psum_scatter(lax.dot_general(attn_out, full_grad, (((0,), (0,)), ((),...  352 us
    all_gather x1, waiting for transfers between devices, local(): lax.all_gather(q_left, 'dp', axis=2, tiled=True)  299 us
    all_gather x1, waiting for transfers between devices, local(): lax.all_gather(q_right, 'dp', axis=1, tiled=True)  281 us
    all_gather x1, waiting for transfers between devices, local(): full_grad = lax.all_gather(out_grad, 'tensor', axis=1, tiled=True)  44.2 us
    all_to_all x1, blocking collectives, local(): lax.all_to_all(both_rows, 'dp', split_axis=1, concat_axis=0, tiled=True)  23.3 us
  transfers between devices with their start and end apart: 5, of which 4 were waited for; matrix products, arithmetic and copies ran while one was open for 2% of the time, Pallas kernels for 0%

commit v1 on v0

v1 whole, which is shorter than its diff:
```python
import jax
import jax.numpy as jnp
from jax import lax
from jax.sharding import Mesh, PartitionSpec as P

STEP = 10


beta_first = 0.9
beta_second = 0.95
adam_eps = 1e-08
learn_rate = 0.1
weight_decay = 0.1

SIZES = {"yh": 2, "core": 2, "zh": 4, "zl": 2, "yl": 2, "x": 4}
Z = ("zh", "zl")
F32, BF16 = jnp.float32, jnp.bfloat16


def adam_step(moment, second, rotated):
    new_moment = beta_first * moment + (1.0 - beta_first) * rotated
    new_second = beta_second * second + (1.0 - beta_second) * rotated * rotated
    first_fix = 1.0 - beta_first**STEP
    second_fix = 1.0 - beta_second**STEP
    normed = new_moment / first_fix / (jnp.sqrt(new_second / second_fix) + adam_eps)
    return (new_moment, new_second, normed)


def shift(value, axes, count, by):
    return lax.ppermute(value, axes, [(i, (i + by) % count) for i in range(count)])


def swap(value, axis):
    return shift(value, axis, 2, 1)


def split(value, dim):
    high = lax.reduce_precision(value, 8, 7)
    low = value - high
    return jnp.concatenate([high.astype(BF16), low.astype(BF16)], axis=dim)


def fold(value):
    half = value.shape[0] // 2
    return value[:half] + value[half:]


def dot(left, right, left_dim, right_dim):
    return lax.dot_general(
        left, right, (((left_dim,), (right_dim,)), ((), ())), preferred_element_type=F32
    )


def ring_sum(parts, axes, count, dim, up):
    here = lax.axis_index(axes)

    def block(offset):
        return lax.dynamic_index_in_dim(parts, (here + offset) % count, dim, keepdims=False)

    down = count - 1 - up
    from_below, from_above = block(up), block(-down)
    for step in range(max(up, down)):
        if step < up:
            from_below = shift(from_below, axes, count, 1)
            if step < up - 1:
                from_below = from_below + block(up - 1 - step)
        if step < down:
            from_above = shift(from_above, axes, count, -1)
            if step < down - 1:
                from_above = from_above + block(-(down - 1 - step))
    return block(0) + from_below + from_above


def local(attn_out, out_grad, q_left, q_right, weight, moment, second):
    yl, yh, core = (lax.axis_index(a) for a in ("yl", "yh", "core"))

    grad_1 = swap(out_grad, "core")
    half = out_grad.shape[1] // 2
    mine = lax.dynamic_slice_in_dim(out_grad, yl * half, half, 1)
    others = lax.dynamic_slice_in_dim(out_grad, (1 - yl) * half, half, 1)
    grad_2 = swap(mine, "yh")
    grad_2y = lax.ppermute(others, ("yh", "yl"), [(i, 3 - i) for i in range(4)])
    attn_y = swap(attn_out, "yl")
    grad_3, grad_3y = swap(grad_2, "core"), swap(grad_2y, "core")

    part_0 = dot(out_grad, attn_out, 0, 0).reshape(2, 4, 128, 1024)
    part_1 = dot(grad_1, attn_out, 0, 0).reshape(2, 4, 128, 1024)
    sum_0 = ring_sum(part_0, "x", 4, 1, 2)
    sum_1 = ring_sum(part_1, "x", 4, 1, 1)
    both = jnp.stack([sum_0, sum_1]).reshape(2, 2, 8, 16, 1024)
    both = ring_sum(both, Z, 8, 2, 4)
    kept = lax.dynamic_index_in_dim(both, yl, 1, keepdims=False)
    given = lax.dynamic_index_in_dim(both, 1 - yl, 1, keepdims=False)
    rows_a = kept + swap(given, "yl")

    part_2 = dot(grad_2, attn_out, 0, 0) + dot(grad_2y, attn_y, 0, 0)
    part_3 = dot(grad_3, attn_out, 0, 0) + dot(grad_3y, attn_y, 0, 0)
    part_b = jnp.stack([part_2, part_3]).reshape(2, 4, 8, 16, 1024)
    rows_b = ring_sum(part_b, Z, 8, 2, 3)
    rows_b = ring_sum(rows_b, "x", 4, 1, 2)
    rows = jnp.concatenate([rows_a, rows_b]).reshape(64, 1024)

    right = q_right[0].reshape(16, 4, 16, 16).transpose(0, 2, 1, 3).reshape(16, 1024)
    right = lax.all_gather(right, ("yl", "x"), axis=0, tiled=True)
    right = lax.all_gather(right, Z, axis=0, tiled=True)
    left = lax.all_to_all(q_left[0], "zh", 0, 0, tiled=True)
    left = lax.all_gather(left, "x", axis=0)
    left = lax.all_gather(left, ("zl", "yl"), axis=0)
    left = left.reshape(16, 4, 16, 1024).transpose(1, 0, 2, 3).reshape(1024, 1024)

    def to_block(value):
        moved = value.reshape(16, 4, 1024).transpose(1, 0, 2)
        return lax.all_to_all(moved, "zh", 0, 0, tiled=True).reshape(64, 1024)

    moment_b, second_b = to_block(moment), to_block(second)

    turned = fold(dot(split(rows, 0), right, 1, 0)).reshape(4, 16, 2, 2, 4, 64)
    turned = jnp.where(core == 1, turned[jnp.array([1, 0, 3, 2])], turned)
    turned = jnp.where(yh == 1, turned[jnp.array([2, 3, 0, 1])], turned)
    turned = turned.transpose(3, 4, 0, 2, 1, 5).reshape(64, 16, 64)
    turned = lax.all_to_all(turned, ("yl", "x", "zh", "zl"), 0, 0, tiled=True).reshape(1024, 64)
    rotated = fold(dot(split(turned, 1), left, 0, 0))
    normed = adam_step(moment_b, second_b, rotated)[2]
    back = fold(dot(split(normed, 0), left, 1, 1)).reshape(64, 16, 64).transpose(1, 0, 2)
    back = lax.all_to_all(back, ("zl", "yl", "x"), 0, 0, tiled=True).reshape(1024, 64)
    unrotated = fold(dot(split(back, 1), right, 0, 1))

    own = lax.all_to_all(rotated.reshape(4, 16, 1024), "zh", 0, 0, tiled=True)
    own = own.transpose(1, 0, 2).reshape(16, 4096)
    new_moment, new_second, _ = adam_step(moment, second, own)
    new_weight = weight - learn_rate * (unrotated + weight_decay * weight)
    return (new_weight, unrotated.astype(BF16), new_moment, new_second)


def solution(mesh):
    fine = Mesh(mesh.devices.reshape(tuple(SIZES.values())), tuple(SIZES))
    tensor, dp = ("yh", "core"), ("zh", "zl", "yl", "x")
    whole = tensor + dp
    return jax.shard_map(
        local,
        mesh=fine,
        in_specs=(
            P(dp, tensor),
            P(dp, tensor),
            P(tensor, None, dp, None),
            P(tensor, dp, None),
            P(dp, tensor),
            P(whole, None),
            P(whole, None),
        ),
        out_specs=(P(dp, tensor), P(dp, tensor), P(whole, None), P(whole, None)),
        check_vma=False,
    )
```

time: 1100 us -> 363 us (0.33)
  waiting for transfers between devices: 979 us -> 121 us
  starting transfers between devices: 13.6 us -> 77.7 us
  blocking collectives: 39.8 us -> 73 us
  other arithmetic: 6.64 us -> 35.8 us
  matrix products: 35.6 us -> 13.2 us
    all_gather x3 -> x2, waiting for transfers between devices: 624 us -> 0.02 us  [the longest x1 0.02 us: local(): right = lax.all_gather(right, Z, axis=0, tiled=True)]
    reduce_scatter x1 -> x0, waiting for transfers between devices: 352 us -> none  [local(): lax.psum_scatter(lax.dot_general(attn_out, full_grad, (((0,), (0,)), ((),...]
    ppermute x0 -> x30, waiting for transfers between devices: none -> 91.6 us  [the longest x29 86.1 us: shift(): lax.ppermute(value, axes, [(i, (i + by) % count) for i in range(count)])]
    all_gather x0 -> x2, blocking collectives: none -> 73 us  [the longest x1 57.9 us: local(): right = lax.all_gather(right, ('yl', 'x'), axis=0, tiled=True)]
    ppermute x0 -> x30, starting transfers between devices: none -> 46.2 us  [the longest x29 44.6 us: shift(): lax.ppermute(value, axes, [(i, (i + by) % count) for i in range(count)])]
    all_to_all x2 -> x0, blocking collectives: 39.8 us -> none  [the longest x1 23.3 us: local(): lax.all_to_all(both_rows, 'dp', split_axis=1, concat_axis=0, tiled=True)]
    all_to_all x1 -> x6, waiting for transfers between devices: 0.01 us -> 28.8 us  [the longest x1 8.82 us: local(): lax.all_to_all(turned, ('yl', 'x', 'zh', 'zl'), 0, 0, tiled=True)]
    add x0 -> x20, other arithmetic: none -> 26.9 us  [the longest x7 12.5 us: ring_sum(): from_below = from_below + block(up - 1 - step)]
  transfers between devices with their start and end apart: 5 -> 38, of which waited for: 4 -> 14; matrix products, arithmetic and copies ran while one was open for 2% -> 17% of each run, Pallas kernels for 0% -> 0%
where the time goes in v1:
time: 363 us; the launch traced here: 357 us
  waiting for transfers between devices  121 us (33%)
  starting transfers between devices  77.7 us (21%)
  blocking collectives  73 us (20%)
  other arithmetic  35.8 us (10%)
  local copies, waits for them, and re-layouts  21.4 us (6%)
  between operations  14.9 us (4%)
  matrix products  13.2 us (4%)
    ppermute x29, waiting for transfers between devices, shift(): lax.ppermute(value, axes, [(i, (i + by) % count) for i in range(count)])  86.1 us
    all_gather x1, blocking collectives, local(): right = lax.all_gather(right, ('yl', 'x'), axis=0, tiled=True)  57.9 us
    ppermute x29, starting transfers between devices, shift(): lax.ppermute(value, axes, [(i, (i + by) % count) for i in range(count)])  44.6 us
    all_to_all x2, starting transfers between devices, to_block(): return lax.all_to_all(moved, 'zh', 0, 0, tiled=True).reshape(64, 1024)  15.5 us
    all_gather x1, blocking collectives, local(): left = lax.all_gather(left, 'x', axis=0)  15.1 us
    dot_general x10, matrix products, dot(): lax.dot_general(left, right, (((left_dim,), (right_dim,)), ((), ())), pre...  13.2 us
    add x7, other arithmetic, ring_sum(): from_below = from_below + block(up - 1 - step)  12.5 us
    all_to_all x1, waiting for transfers between devices, local(): lax.all_to_all(turned, ('yl', 'x', 'zh', 'zl'), 0, 0, tiled=True)  8.82 us
  transfers between devices with their start and end apart: 38, of which 14 were waited for; matrix products, arithmetic and copies ran while one was open for 17% of the time, Pallas kernels for 0%

profile of v1, /device:TPU:8, one launch (start us, length us, event | category | flops | bytes accessed | tf_op | source)
XLA Modules:
  0.0 356.5 jit_solution(15540374769929521659)
XLA Ops:
  7.3 2.4 constant_dynamic-slice_fusion.1
  11.4 1.9 collective-permute-start.17
  18.7 5.5 %collective-permute-done.16 = bf16[512,512]{1,0:T(8,128)(2,1)} collective-permute-done((bf16[512,512]{1,0:T(8,128)(2,1)}, bf16[512,512]{1,0:T(8,128)(2,1)}, u32[]{:S(2)}, u32[]{:S(2)}) %collective-permute-start.16) | collective-permute-done | bytes 524320 | tf_op jit(solution)/shard_map/ppermute | solution.py:82
  24.2 24.5 %collective-permute-done.15 = bf16[512,512]{1,0:T(8,128)(2,1)} collective-permute-done((bf16[512,512]{1,0:T(8,128)(2,1)}, bf16[512,512]{1,0:T(8,128)(2,1)}, u32[]{:S(2)}, u32[]{:S(2)}) %collective-permute-start.15) | collective-permute-done | bytes 524320 | tf_op jit(solution)/shard_map/ppermute | solution.py:30
  48.7 2.5 fusion.83
  53.9 1.7 collective-permute-start.5
  56.6 1.8 fusion.84
  58.3 1.9 convolution_add_fusion.1
  63.5 1.9 collective-permute-start.20
  68.6 57.9 %all_gather.18 = bf16[128,1024]{1,0:T(8,128)(2,1)} all-gather(bf16[16,1024]{1,0:T(8,128)(2,1)S(1)} %reshape.73), channel_id=1, replica_groups=mesh['yh'=2,'core'=2,'zh'=4,'zl'=2,'yl'=2,'x'=4] {'yl','x'}, dimensions={0}, use_global_device_ids=true | all-gather | bytes 294912 | tf_op jit(solution)/shard_map/all_gather | solution.py:104
  126.6 2.8 bitcast_add_fusion.2
  131.0 5.9 %collective-permute-start.23 = (f32[2,4,16,1024]{3,2,1,0:T(8,128)}, f32[2,4,16,1024]{3,2,1,0:T(8,128)}, u32[]{:S(2)}, u32[]{:S(2)}) collective-permute-start(f32[2,4,16,1024]{3,2,1,0:T(8,128)} %get-tuple-element.14), channel_id=1, source_target_pairs={{0,56},{8,0},{16,8},{24,16},{32,24},{40,32},{48,40},{56,48},{1,57}... | collective-permute-start | bytes 1572872 | tf_op jit(solution)/shard_map/ppermute | solution.py:30
  136.9 1.9 fusion.14
  138.9 2.9 bitcast_add_fusion
  141.8 5.2 %collective-permute-done.23 = f32[2,4,16,1024]{3,2,1,0:T(8,128)} collective-permute-done((f32[2,4,16,1024]{3,2,1,0:T(8,128)}, f32[2,4,16,1024]{3,2,1,0:T(8,128)}, u32[]{:S(2)}, u32[]{:S(2)}) %collective-permute-start.23) | collective-permute-done | bytes 524320 | tf_op jit(solution)/shard_map/ppermute | solution.py:30
  148.6 7.3 %collective-permute-done.21 = f32[2,4,16,1024]{3,2,1,0:T(8,128)} collective-permute-done((f32[2,4,16,1024]{3,2,1,0:T(8,128)}, f32[2,4,16,1024]{3,2,1,0:T(8,128)}, u32[]{:S(2)}, u32[]{:S(2)}) %collective-permute-start.21) | collective-permute-done | bytes 524320 | tf_op jit(solution)/shard_map/ppermute | solution.py:30
  155.9 2.3 fusion.17
  158.2 2.3 fusion.1
  160.5 20.1 %collective-permute-done.24 = f32[2,4,16,1024]{3,2,1,0:T(8,128)} collective-permute-done((f32[2,4,16,1024]{3,2,1,0:T(8,128)}, f32[2,4,16,1024]{3,2,1,0:T(8,128)}, u32[]{:S(2)}, u32[]{:S(2)}) %collective-permute-start.24) | collective-permute-done | bytes 524320 | tf_op jit(solution)/shard_map/ppermute | solution.py:30
  180.7 1.9 fusion.25
  183.8 2.1 fusion
  187.6 10.0 %collective-permute-done.7 = f32[2,2,16,1024]{3,2,1,0:T(8,128)S(1)} collective-permute-done((f32[2,2,16,1024]{3,2,1,0:T(8,128)S(1)}, f32[2,2,16,1024]{3,2,1,0:T(8,128)S(1)}, u32[]{:S(2)}, u32[]{:S(2)}) %collective-permute-start.7) | collective-permute-done | bytes 262176 | tf_op jit(solution)/shard_map/ppermute | solution.py:30
  198.4 3.3 all-to-all-start.2
  202.5 2.6 collective-permute-start.22
  205.0 2.7 collective-permute-start.11
  207.7 2.0 fusion.5
  209.7 2.0 collective-permute-start.26
  211.7 1.7 fusion.49
  213.4 5.1 %all-to-all-start.3 = ((f32[4,16,1024]{2,1,0:T(8,128)}), f32[4,16,1024]{2,1,0:T(8,128)}, u32[]{:S(2)}, u32[]{:S(2)}) async-start(f32[4,16,1024]{2,1,0:T(8,128)} %bitcast.207), calls=%async_computation.3 | async-start | bytes 524288 | tf_op jit(solution)/shard_map/all_to_all | solution.py:113
  218.6 15.1 %all-gather = bf16[16,16,1024]{2,1,0:T(8,128)(2,1)} all-gather(bf16[4,16,1024]{2,1,0:T(8,128)(2,1)S(1)} %all-to-all-done.2), channel_id=2, replica_groups=mesh['yh'=2,'core'=2,'zh'=4,'zl'=2,'yl'=2,'x'=4] {'x'}, dimensions={0}, use_global_device_ids=true | all-gather | bytes 655360 | tf_op jit(solution)/shard_map/all_gather | solution.py:107
  233.7 2.1 fusion.52
  235.7 12.8 %collective-permute-start.12 = (f32[2,2,16,1024]{3,2,1,0:T(8,128)S(1)}, f32[2,2,16,1024]{3,2,1,0:T(8,128)S(1)}, u32[]{:S(2)}, u32[]{:S(2)}) collective-permute-start(f32[2,2,16,1024]{3,2,1,0:T(8,128)S(1)} %get-tuple-element.16), channel_id=1, source_target_pairs={{0,56},{8,0},{16,8},{24,16},{32,24},{40,32},{48,40},{56,48},{1,57}... | collective-permute-start | bytes 786440 | tf_op jit(solution)/shard_map/ppermute | solution.py:30
  250.8 6.6 %collective-permute-done.12 = f32[2,2,16,1024]{3,2,1,0:T(8,128)S(1)} collective-permute-done((f32[2,2,16,1024]{3,2,1,0:T(8,128)S(1)}, f32[2,2,16,1024]{3,2,1,0:T(8,128)S(1)}, u32[]{:S(2)}, u32[]{:S(2)}) %collective-permute-start.12) | collective-permute-done | bytes 262176 | tf_op jit(solution)/shard_map/ppermute | solution.py:30
  257.4 2.9 collective-permute-start.13
  262.0 2.1 collective-permute-start.28
  264.1 2.9 collective-permute-done.13
  269.2 8.4 %collective-permute-done.14 = f32[2,16,1024]{2,1,0:T(8,128)S(1)} collective-permute-done((f32[2,16,1024]{2,1,0:T(8,128)S(1)}, f32[2,16,1024]{2,1,0:T(8,128)S(1)}, u32[]{:S(2)}, u32[]{:S(2)}) %collective-permute-start.14) | collective-permute-done | bytes 131104 | tf_op jit(solution)/shard_map/ppermute | solution.py:30
  277.7 2.0 fusion.58
  280.9 10.4 %all-to-all-start = ((f32[4,16,1024]{2,1,0:T(8,128)}), f32[4,16,1024]{2,1,0:T(8,128)S(1)}, u32[]{:S(2)}, u32[]{:S(2)}) async-start(f32[4,16,1024]{2,1,0:T(8,128)} %bitcast.166), calls=%async_computation | async-start | bytes 524288 | tf_op jit(solution)/shard_map/all_to_all | solution.py:113
  293.2 7.4 %all-to-all-done = f32[4,16,1024]{2,1,0:T(8,128)S(1)} async-done(((f32[4,16,1024]{2,1,0:T(8,128)}), f32[4,16,1024]{2,1,0:T(8,128)S(1)}, u32[]{:S(2)}, u32[]{:S(2)}) %all-to-all-start) | async-done | bytes 262176 | tf_op jit(solution)/shard_map/all_to_all | solution.py:113
  300.6 5.1 %all-to-all-start.1 = ((f32[64,1,1024]{2,1,0:T(1,128)}), f32[64,1,1024]{2,1,0:T(1,128)S(1)}, u32[]{:S(2)}, u32[]{:S(2)}) async-start(f32[64,1,1024]{2,1,0:T(1,128)} %reshape.103), calls=%async_computation.1 | async-start | bytes 524288 | tf_op jit(solution)/shard_map/all_to_all | solution.py:121
  305.8 1.7 broadcast_multiply_fusion
  308.2 1.8 copy.39
  309.9 8.8 %all-to-all-done.1 = f32[64,1,1024]{2,1,0:T(1,128)S(1)} async-done(((f32[64,1,1024]{2,1,0:T(1,128)}), f32[64,1,1024]{2,1,0:T(1,128)S(1)}, u32[]{:S(2)}, u32[]{:S(2)}) %all-to-all-start.1) | async-done | bytes 262176 | tf_op jit(solution)/shard_map/all_to_all | solution.py:121
  322.6 3.4 all-to-all-start.5
  328.1 6.9 %all-to-all-done.5 = f32[4,16,1024]{2,1,0:T(8,128)S(1)} async-done(((f32[4,16,1024]{2,1,0:T(8,128)}), f32[4,16,1024]{2,1,0:T(8,128)S(1)}, u32[]{:S(2)}, u32[]{:S(2)}) %all-to-all-start.5) | async-done | bytes 262176 | tf_op jit(solution)/shard_map/all_to_all | solution.py:128
  335.1 4.1 %all-to-all-start.4 = ((f32[16,1,4096]{2,1,0:T(1,128)}), f32[16,1,4096]{2,1,0:T(1,128)S(1)}, u32[]{:S(2)}, u32[]{:S(2)}) async-start(f32[16,1,4096]{2,1,0:T(1,128)} %reshape.105), calls=%async_computation.4 | async-start | bytes 524288 | tf_op jit(solution)/shard_map/all_to_all | solution.py:125
  340.1 5.7 %all-to-all-done.4 = f32[16,1,4096]{2,1,0:T(1,128)S(1)} async-done(((f32[16,1,4096]{2,1,0:T(1,128)}), f32[16,1,4096]{2,1,0:T(1,128)S(1)}, u32[]{:S(2)}, u32[]{:S(2)}) %all-to-all-start.4) | async-done | bytes 262176 | tf_op jit(solution)/shard_map/all_to_all | solution.py:125
  (158 shorter events, 45.1 us)
Async XLA Ops:
  7.2 270.5 %all-gather.5.cloned.1.call-start = ((), (), s32[]{:S(2)}) async-start(), calls=%async_computation.6 | async-start | bytes 2359296 | tf_op jit(solution)/shard_map/all_gather | solution.py:105
  7.2 41.5 %collective-permute-start.3 = (bf16[512,1024]{1,0:T(8,128)(2,1)}, bf16[512,1024]{1,0:T(8,128)(2,1)}, u32[]{:S(2)}, u32[]{:S(2)}) collective-permute-start(bf16[512,1024]{1,0:T(8,128)(2,1)} %param.10), channel_id=1, source_target_pairs={{0,64},{64,0},{1,65},{65,1},{2,66},{66,2},{3,67},{67,3},{4,68},{68... | collective-permute-start | bytes 3145736 | tf_op jit(solution)/shard_map/ppermute | solution.py:30
  9.8 14.4 %collective-permute-start.16 = (bf16[512,512]{1,0:T(8,128)(2,1)}, bf16[512,512]{1,0:T(8,128)(2,1)}, u32[]{:S(2)}, u32[]{:S(2)}) collective-permute-start(bf16[512,512]{1,0:T(8,128)(2,1)} %get-tuple-element.20), channel_id=1, source_target_pairs={{0,132},{4,128},{128,4},{132,0},{1,133},{5,129},{129,5},{133,1},{2... | collective-permute-start | bytes 1572872 | tf_op jit(solution)/shard_map/ppermute | solution.py:82
  11.4 44.2 %collective-permute-start.17 = (bf16[512,1024]{1,0:T(8,128)(2,1)S(1)}, bf16[512,1024]{1,0:T(8,128)(2,1)S(1)}, u32[]{:S(2)}, u32[]{:S(2)}) collective-permute-start(bf16[512,1024]{1,0:T(8,128)(2,1)S(1)} %copy-done.11), channel_id=1, source_target_pairs={{0,4},{4,0},{1,5},{5,1},{2,6},{6,2},{3,7},{7,3},{8,12},{12,8},{9,1... | collective-permute-start | bytes 3145736 | tf_op jit(solution)/shard_map/ppermute | solution.py:30
  13.2 35.5 %collective-permute-start.15 = (bf16[512,512]{1,0:T(8,128)(2,1)}, bf16[512,512]{1,0:T(8,128)(2,1)}, u32[]{:S(2)}, u32[]{:S(2)}) collective-permute-start(bf16[512,512]{1,0:T(8,128)(2,1)} %get-tuple-element.19), channel_id=1, source_target_pairs={{0,128},{128,0},{1,129},{129,1},{2,130},{130,2},{3,131},{131,3},{4... | collective-permute-start | bytes 1572872 | tf_op jit(solution)/shard_map/ppermute | solution.py:30
  18.0 108.6 %collective-permute-start = (f32[2,128,1024]{2,1,0:T(8,128)}, f32[2,128,1024]{2,1,0:T(8,128)}, u32[]{:S(2)}, u32[]{:S(2)}) collective-permute-start(f32[2,128,1024]{2,1,0:T(8,128)} %get-tuple-element.9), channel_id=1, source_target_pairs={{0,1},{1,2},{2,3},{3,0},{4,5},{5,6},{6,7},{7,4},{8,9},{9,10},{10,1... | collective-permute-start | bytes 3145736 | tf_op jit(solution)/shard_map/ppermute | solution.py:30
  24.2 36.0 %collective-permute-start.19 = (bf16[512,512]{1,0:T(8,128)(2,1)}, bf16[512,512]{1,0:T(8,128)(2,1)S(1)}, u32[]{:S(2)}, u32[]{:S(2)}) collective-permute-start(bf16[512,512]{1,0:T(8,128)(2,1)} %collective-permute-done.16), channel_id=1, source_target_pairs={{0,64},{64,0},{1,65},{65,1},{2,66},{66,2},{3,67},{67,3},{4,68},{68... | collective-permute-start | bytes 1572872 | tf_op jit(solution)/shard_map/ppermute | solution.py:30
  48.7 12.3 %collective-permute-start.18 = (bf16[512,512]{1,0:T(8,128)(2,1)}, bf16[512,512]{1,0:T(8,128)(2,1)S(1)}, u32[]{:S(2)}, u32[]{:S(2)}) collective-permute-start(bf16[512,512]{1,0:T(8,128)(2,1)} %collective-permute-done.15), channel_id=1, source_target_pairs={{0,64},{64,0},{1,65},{65,1},{2,66},{66,2},{3,67},{67,3},{4,68},{68... | collective-permute-start | bytes 1572872 | tf_op jit(solution)/shard_map/ppermute | solution.py:30
  53.9 85.0 %collective-permute-start.5 = (f32[2,128,1024]{2,1,0:T(8,128)}, f32[2,128,1024]{2,1,0:T(8,128)}, u32[]{:S(2)}, u32[]{:S(2)}) collective-permute-start(f32[2,128,1024]{2,1,0:T(8,128)} %get-tuple-element.8), channel_id=1, source_target_pairs={{0,3},{1,0},{2,1},{3,2},{4,7},{5,4},{6,5},{7,6},{8,11},{9,8},{10,9... | collective-permute-start | bytes 3145736 | tf_op jit(solution)/shard_map/ppermute | solution.py:30
  63.5 73.4 %collective-permute-start.20 = (f32[2,4,16,1024]{3,2,1,0:T(8,128)}, f32[2,4,16,1024]{3,2,1,0:T(8,128)}, u32[]{:S(2)}, u32[]{:S(2)}) collective-permute-start(f32[2,4,16,1024]{3,2,1,0:T(8,128)} %get-tuple-element.13), channel_id=1, source_target_pairs={{0,8},{8,16},{16,24},{24,32},{32,40},{40,48},{48,56},{56,0},{1,9},... | collective-permute-start | bytes 1572872 | tf_op jit(solution)/shard_map/ppermute | solution.py:30
  65.4 92.8 %collective-permute-start.2 = (f32[2,128,1024]{2,1,0:T(8,128)S(1)}, f32[2,128,1024]{2,1,0:T(8,128)}, u32[]{:S(2)}, u32[]{:S(2)}) collective-permute-start(f32[2,128,1024]{2,1,0:T(8,128)S(1)} %copy-done.17), channel_id=1, source_target_pairs={{0,3},{1,0},{2,1},{3,2},{4,7},{5,4},{6,5},{7,6},{8,11},{9,8},{10,9... | collective-permute-start | bytes 3145736 | tf_op jit(solution)/shard_map/ppermute | solution.py:30
  129.4 28.8 %collective-permute-start.1 = (f32[2,128,1024]{2,1,0:T(8,128)}, f32[2,128,1024]{2,1,0:T(8,128)}, u32[]{:S(2)}, u32[]{:S(2)}) collective-permute-start(f32[2,128,1024]{2,1,0:T(8,128)} %bitcast_add_fusion.2), channel_id=1, source_target_pairs={{0,1},{1,2},{2,3},{3,0},{4,5},{5,6},{6,7},{7,4},{8,9},{9,10},{10,1... | collective-permute-start | bytes 3145736 | tf_op jit(solution)/shard_map/ppermute | solution.py:30
  131.0 16.0 %collective-permute-start.23 = (f32[2,4,16,1024]{3,2,1,0:T(8,128)}, f32[2,4,16,1024]{3,2,1,0:T(8,128)}, u32[]{:S(2)}, u32[]{:S(2)}) collective-permute-start(f32[2,4,16,1024]{3,2,1,0:T(8,128)} %get-tuple-element.14), channel_id=1, source_target_pairs={{0,56},{8,0},{16,8},{24,16},{32,24},{40,32},{48,40},{56,48},{1,57}... | collective-permute-start | bytes 1572872 | tf_op jit(solution)/shard_map/ppermute | solution.py:30
  138.8 17.1 %collective-permute-start.21 = (f32[2,4,16,1024]{3,2,1,0:T(8,128)}, f32[2,4,16,1024]{3,2,1,0:T(8,128)}, u32[]{:S(2)}, u32[]{:S(2)}) collective-permute-start(f32[2,4,16,1024]{3,2,1,0:T(8,128)} %fusion.14), channel_id=1, source_target_pairs={{0,8},{8,16},{16,24},{24,32},{32,40},{40,48},{48,56},{56,0},{1,9},... | collective-permute-start | bytes 1572872 | tf_op jit(solution)/shard_map/ppermute | solution.py:30
  138.8 17.1 %copy-start.2 = (f32[512,1024]{1,0:T(8,128)S(1)}, f32[512,1024]{1,0:T(8,128)}, u32[]{:S(2)}) copy-start(f32[512,1024]{1,0:T(8,128)} %copy-done) | copy-start | bytes 6291460
  138.8 44.9 %collective-permute-start.4 = (f32[2,128,1024]{2,1,0:T(8,128)}, f32[2,128,1024]{2,1,0:T(8,128)}, u32[]{:S(2)}, u32[]{:S(2)}) collective-permute-start(f32[2,128,1024]{2,1,0:T(8,128)} %get-tuple-element.7), channel_id=1, source_target_pairs={{0,1},{1,2},{2,3},{3,0},{4,5},{5,6},{6,7},{7,4},{8,9},{9,10},{10,1... | collective-permute-start | bytes 3145736 | tf_op jit(solution)/shard_map/ppermute | solution.py:30
  147.0 36.8 %collective-permute-start.6 = (f32[2,128,1024]{2,1,0:T(8,128)}, f32[2,128,1024]{2,1,0:T(8,128)}, u32[]{:S(2)}, u32[]{:S(2)}) collective-permute-start(f32[2,128,1024]{2,1,0:T(8,128)} %bitcast_add_fusion), channel_id=1, source_target_pairs={{0,3},{1,0},{2,1},{3,2},{4,7},{5,4},{6,5},{7,6},{8,11},{9,8},{10,9... | collective-permute-start | bytes 3145736 | tf_op jit(solution)/shard_map/ppermute | solution.py:30
  158.2 22.5 %collective-permute-start.24 = (f32[2,4,16,1024]{3,2,1,0:T(8,128)}, f32[2,4,16,1024]{3,2,1,0:T(8,128)}, u32[]{:S(2)}, u32[]{:S(2)}) collective-permute-start(f32[2,4,16,1024]{3,2,1,0:T(8,128)} %get-tuple-element.12), channel_id=1, source_target_pairs={{0,56},{8,0},{16,8},{24,16},{32,24},{40,32},{48,40},{56,48},{1,57}... | collective-permute-start | bytes 1572872 | tf_op jit(solution)/shard_map/ppermute | solution.py:30
  158.2 22.5 %copy-start.3 = (f32[512,1024]{1,0:T(8,128)S(1)}, f32[512,1024]{1,0:T(8,128)}, u32[]{:S(2)}) copy-start(f32[512,1024]{1,0:T(8,128)} %copy-done) | copy-start | bytes 6291460
  182.6 25.1 %collective-permute-start.25 = (f32[2,4,16,1024]{3,2,1,0:T(8,128)}, f32[2,4,16,1024]{3,2,1,0:T(8,128)}, u32[]{:S(2)}, u32[]{:S(2)}) collective-permute-start(f32[2,4,16,1024]{3,2,1,0:T(8,128)} %fusion.25), channel_id=1, source_target_pairs={{0,56},{8,0},{16,8},{24,16},{32,24},{40,32},{48,40},{56,48},{1,57}... | collective-permute-start | bytes 1572872 | tf_op jit(solution)/shard_map/ppermute | solution.py:30
  185.9 12.5 %copy-start.5 = (f32[2,128,1024]{2,1,0:T(8,128)}, f32[2,128,1024]{2,1,0:T(8,128)S(1)}, u32[]{:S(2)}) copy-start(f32[2,128,1024]{2,1,0:T(8,128)S(1)} %fusion) | copy-start | bytes 3145732
  186.7 15.0 %copy-start.18 = (f32[16,4096]{1,0:T(8,128)S(1)}, f32[16,4096]{1,0:T(8,128)}, u32[]{:S(2)}) copy-start(f32[16,4096]{1,0:T(8,128)} %param.15) | copy-start | bytes 786436
  186.7 10.9 %collective-permute-start.7 = (f32[2,2,16,1024]{3,2,1,0:T(8,128)S(1)}, f32[2,2,16,1024]{3,2,1,0:T(8,128)S(1)}, u32[]{:S(2)}, u32[]{:S(2)}) collective-permute-start(f32[2,2,16,1024]{3,2,1,0:T(8,128)S(1)} %get-tuple-element.17), channel_id=1, source_target_pairs={{0,8},{8,16},{16,24},{24,32},{32,40},{40,48},{48,56},{56,0},{1,9},... | collective-permute-start | bytes 786440 | tf_op jit(solution)/shard_map/ppermute | solution.py:30
  198.3 13.4 %collective-permute-start.8 = (f32[2,2,16,1024]{3,2,1,0:T(8,128)}, f32[2,2,16,1024]{3,2,1,0:T(8,128)}, u32[]{:S(2)}, u32[]{:S(2)}) collective-permute-start(f32[2,2,16,1024]{3,2,1,0:T(8,128)} %fusion.46), channel_id=1, source_target_pairs={{0,8},{8,16},{16,24},{24,32},{32,40},{40,48},{48,56},{56,0},{1,9},... | collective-permute-start | bytes 786440 | tf_op jit(solution)/shard_map/ppermute | solution.py:30
  198.4 15.1 %all-to-all-start.2 = ((bf16[4,16,1024]{2,1,0:T(8,128)(2,1)}), bf16[4,16,1024]{2,1,0:T(8,128)(2,1)S(1)}, u32[]{:S(2)}, u32[]{:S(2)}) async-start(bf16[4,16,1024]{2,1,0:T(8,128)(2,1)} %bitcast.210), calls=%async_computation.2 | async-start | bytes 262144 | tf_op jit(solution)/shard_map/all_to_all | solution.py:106
  202.5 46.1 %collective-permute-start.22 = (f32[2,4,16,1024]{3,2,1,0:T(8,128)}, f32[2,4,16,1024]{3,2,1,0:T(8,128)}, u32[]{:S(2)}, u32[]{:S(2)}) collective-permute-start(f32[2,4,16,1024]{3,2,1,0:T(8,128)} %get-tuple-element.11), channel_id=1, source_target_pairs={{0,8},{8,16},{16,24},{24,32},{32,40},{40,48},{48,56},{56,0},{1,9},... | collective-permute-start | bytes 1572872 | tf_op jit(solution)/shard_map/ppermute | solution.py:30
  205.0 28.6 %collective-permute-start.11 = (f32[2,2,16,1024]{3,2,1,0:T(8,128)}, f32[2,2,16,1024]{3,2,1,0:T(8,128)}, u32[]{:S(2)}, u32[]{:S(2)}) collective-permute-start(f32[2,2,16,1024]{3,2,1,0:T(8,128)} %get-tuple-element.18), channel_id=1, source_target_pairs={{0,56},{8,0},{16,8},{24,16},{32,24},{40,32},{48,40},{56,48},{1,57}... | collective-permute-start | bytes 786440 | tf_op jit(solution)/shard_map/ppermute | solution.py:30
  209.7 38.9 %collective-permute-start.26 = (f32[2,4,16,1024]{3,2,1,0:T(8,128)}, f32[2,4,16,1024]{3,2,1,0:T(8,128)}, u32[]{:S(2)}, u32[]{:S(2)}) collective-permute-start(f32[2,4,16,1024]{3,2,1,0:T(8,128)} %fusion.5), channel_id=1, source_target_pairs={{0,56},{8,0},{16,8},{24,16},{32,24},{40,32},{48,40},{56,48},{1,57}... | collective-permute-start | bytes 1572872 | tf_op jit(solution)/shard_map/ppermute | solution.py:30
  213.4 20.2 %collective-permute-start.9 = (f32[2,2,16,1024]{3,2,1,0:T(8,128)}, f32[2,2,16,1024]{3,2,1,0:T(8,128)}, u32[]{:S(2)}, u32[]{:S(2)}) collective-permute-start(f32[2,2,16,1024]{3,2,1,0:T(8,128)} %fusion.49), channel_id=1, source_target_pairs={{0,8},{8,16},{16,24},{24,32},{32,40},{40,48},{48,56},{56,0},{1,9},... | collective-permute-start | bytes 786440 | tf_op jit(solution)/shard_map/ppermute | solution.py:30
  213.4 67.5 %all-to-all-start.3 = ((f32[4,16,1024]{2,1,0:T(8,128)}), f32[4,16,1024]{2,1,0:T(8,128)}, u32[]{:S(2)}, u32[]{:S(2)}) async-start(f32[4,16,1024]{2,1,0:T(8,128)} %bitcast.207), calls=%async_computation.3 | async-start | bytes 524288 | tf_op jit(solution)/shard_map/all_to_all | solution.py:113
  218.6 89.6 %all-gather.7.cloned.1.call-start = ((), (), s32[]{:S(2)}) async-start(), calls=%async_computation.7 | async-start | bytes 2621440 | tf_op jit(solution)/shard_map/all_gather | solution.py:108
  233.6 14.9 %copy-start.4 = (f32[512,1024]{1,0:T(8,128)S(1)}, f32[512,1024]{1,0:T(8,128)}, u32[]{:S(2)}) copy-start(f32[512,1024]{1,0:T(8,128)} %copy-done) | copy-start | bytes 6291460
  235.7 21.6 %copy-start.7 = (f32[2,128,1024]{2,1,0:T(8,128)S(1)}, f32[2,128,1024]{2,1,0:T(8,128)}, u32[]{:S(2)}) copy-start(f32[2,128,1024]{2,1,0:T(8,128)} %copy-done.5) | copy-start | bytes 3145732
  235.7 21.6 %collective-permute-start.12 = (f32[2,2,16,1024]{3,2,1,0:T(8,128)S(1)}, f32[2,2,16,1024]{3,2,1,0:T(8,128)S(1)}, u32[]{:S(2)}, u32[]{:S(2)}) collective-permute-start(f32[2,2,16,1024]{3,2,1,0:T(8,128)S(1)} %get-tuple-element.16), channel_id=1, source_target_pairs={{0,56},{8,0},{16,8},{24,16},{32,24},{40,32},{48,40},{56,48},{1,57}... | collective-permute-start | bytes 786440 | tf_op jit(solution)/shard_map/ppermute | solution.py:30
  249.9 10.4 %copy-start.25 = (s32[4]{0:T(128)S(1)}, s32[4]{0:T(128)}, u32[]{:S(2)}) copy-start(s32[4]{0:T(128)} %constant.253) | copy-start | bytes 52
  249.9 10.5 %copy-start.19 = (f32[16,4096]{1,0:T(8,128)S(1)}, f32[16,4096]{1,0:T(8,128)}, u32[]{:S(2)}) copy-start(f32[16,4096]{1,0:T(8,128)} %param.14) | copy-start | bytes 786436
  249.9 17.1 %copy-start.8 = (f32[2,128,1024]{2,1,0:T(8,128)S(1)}, f32[2,128,1024]{2,1,0:T(8,128)}, u32[]{:S(2)}) copy-start(f32[2,128,1024]{2,1,0:T(8,128)} %copy-done.5) | copy-start | bytes 3145732
  250.6 10.5 %collective-permute-start.27 = (f32[2,16,1024]{2,1,0:T(8,128)}, f32[2,16,1024]{2,1,0:T(8,128)S(1)}, u32[]{:S(2)}, u32[]{:S(2)}) collective-permute-start(f32[2,16,1024]{2,1,0:T(8,128)} %get-tuple-element.25), channel_id=1, source_target_pairs={{0,1},{1,2},{2,3},{3,0},{4,5},{5,6},{6,7},{7,4},{8,9},{9,10},{10,1... | collective-permute-start | bytes 393224 | tf_op jit(solution)/shard_map/ppermute | solution.py:30
  250.8 13.4 %collective-permute-start.10 = (f32[2,2,16,1024]{3,2,1,0:T(8,128)}, f32[2,2,16,1024]{3,2,1,0:T(8,128)S(1)}, u32[]{:S(2)}, u32[]{:S(2)}) collective-permute-start(f32[2,2,16,1024]{3,2,1,0:T(8,128)} %get-tuple-element.15), channel_id=1, source_target_pairs={{0,8},{8,16},{16,24},{24,32},{32,40},{40,48},{48,56},{56,0},{1,9},... | collective-permute-start | bytes 786440 | tf_op jit(solution)/shard_map/ppermute | solution.py:30
  257.4 9.6 %collective-permute-start.13 = (f32[2,2,16,1024]{3,2,1,0:T(8,128)S(1)}, f32[2,2,16,1024]{3,2,1,0:T(8,128)S(1)}, u32[]{:S(2)}, u32[]{:S(2)}) collective-permute-start(f32[2,2,16,1024]{3,2,1,0:T(8,128)S(1)} %fusion.37), channel_id=1, source_target_pairs={{0,56},{8,0},{16,8},{24,16},{32,24},{40,32},{48,40},{56,48},{1,57}... | collective-permute-start | bytes 786440 | tf_op jit(solution)/shard_map/ppermute | solution.py:30
  261.1 6.3 %collective-permute-start.29 = (f32[2,16,1024]{2,1,0:T(8,128)}, f32[2,16,1024]{2,1,0:T(8,128)S(1)}, u32[]{:S(2)}, u32[]{:S(2)}) collective-permute-start(f32[2,16,1024]{2,1,0:T(8,128)} %get-tuple-element.26), channel_id=1, source_target_pairs={{0,3},{1,0},{2,1},{3,2},{4,7},{5,4},{6,5},{7,6},{8,11},{9,8},{10,9... | collective-permute-start | bytes 393224 | tf_op jit(solution)/shard_map/ppermute | solution.py:30
  262.0 6.3 %collective-permute-start.28 = (f32[2,16,1024]{2,1,0:T(8,128)S(1)}, f32[2,16,1024]{2,1,0:T(8,128)S(1)}, u32[]{:S(2)}, u32[]{:S(2)}) collective-permute-start(f32[2,16,1024]{2,1,0:T(8,128)S(1)} %bitcast_add_fusion.5), channel_id=1, source_target_pairs={{0,1},{1,2},{2,3},{3,0},{4,5},{5,6},{6,7},{7,4},{8,9},{9,10},{10,1... | collective-permute-start | bytes 393224 | tf_op jit(solution)/shard_map/ppermute | solution.py:30
  267.1 10.5 %collective-permute-start.14 = (f32[2,16,1024]{2,1,0:T(8,128)S(1)}, f32[2,16,1024]{2,1,0:T(8,128)S(1)}, u32[]{:S(2)}, u32[]{:S(2)}) collective-permute-start(f32[2,16,1024]{2,1,0:T(8,128)S(1)} %dynamic-slice_bitcast_fusion.6), channel_id=1, source_target_pairs={{0,4},{4,0},{1,5},{5,1},{2,6},{6,2},{3,7},{7,3},{8,12},{12,8},{9,1... | collective-permute-start | bytes 393224 | tf_op jit(solution)/shard_map/ppermute | solution.py:30
  280.9 19.7 %all-to-all-start = ((f32[4,16,1024]{2,1,0:T(8,128)}), f32[4,16,1024]{2,1,0:T(8,128)S(1)}, u32[]{:S(2)}, u32[]{:S(2)}) async-start(f32[4,16,1024]{2,1,0:T(8,128)} %bitcast.166), calls=%async_computation | async-start | bytes 524288 | tf_op jit(solution)/shard_map/all_to_all | solution.py:113
  300.6 18.1 %all-to-all-start.1 = ((f32[64,1,1024]{2,1,0:T(1,128)}), f32[64,1,1024]{2,1,0:T(1,128)S(1)}, u32[]{:S(2)}, u32[]{:S(2)}) async-start(f32[64,1,1024]{2,1,0:T(1,128)} %reshape.103), calls=%async_computation.1 | async-start | bytes 524288 | tf_op jit(solution)/shard_map/all_to_all | solution.py:121
  322.6 12.5 %all-to-all-start.5 = ((f32[4,16,1024]{2,1,0:T(8,128)}), f32[4,16,1024]{2,1,0:T(8,128)S(1)}, u32[]{:S(2)}, u32[]{:S(2)}) async-start(f32[4,16,1024]{2,1,0:T(8,128)} %bitcast.51), calls=%async_computation.5 | async-start | bytes 524288 | tf_op jit(solution)/shard_map/all_to_all | solution.py:128
  326.9 12.4 %copy-start.20 = (f32[16,4096]{1,0:T(8,128)S(1)}, f32[16,4096]{1,0:T(8,128)}, u32[]{:S(2)}) copy-start(f32[16,4096]{1,0:T(8,128)} %param.14) | copy-start | bytes 786436
  335.1 10.7 %all-to-all-start.4 = ((f32[16,1,4096]{2,1,0:T(1,128)}), f32[16,1,4096]{2,1,0:T(1,128)S(1)}, u32[]{:S(2)}, u32[]{:S(2)}) async-start(f32[16,1,4096]{2,1,0:T(1,128)} %reshape.105), calls=%async_computation.4 | async-start | bytes 524288 | tf_op jit(solution)/shard_map/all_to_all | solution.py:125
  (17 other events, 68.3 us)
Sparse Core Ops, SparseCore 0:
  126.7 54.1 all-gather.4
  233.8 51.2 all-gather.6
